TPU v7x, 32 devices: a whole 2x2x4 slice. The times are simulated.
32 devices in a mesh: bead: 2 (over y), orb: 4 (over z), fit: 4 (over x, core).
Axes of the slice: x: 2, y: 2, z: 4, core: 2. Of those that a mesh axis runs over, the one named last changes fastest.
Arguments:
- half_ints: bfloat16 [8, 32, 128, 2432], P(('bead', 'orb'), 'fit'), parts along dimension 0, may hold values from -0.0625 to 0.0625
- orbital_coeffs: bfloat16 [8, 512, 128], P(('bead', 'orb')), parts along dimension 0, may hold values from -6 to 6
- block_owner: int32 [8], P('bead'), parts along dimension 0, may hold values from 0 to 3, as said below
- dom_start: int32 [8], P('bead'), parts along dimension 0, may hold values from 0 to 1407, as said below
- pair_list: int32 [20, 2], P('bead'), parts along dimension 0, may hold values from 0 to 3, as said below
Outputs:
- exch: float32 [8, 512, 128], P(('bead', 'orb'), 'fit'), parts along dimension 0
There are 2 independent parts, one for each index of `bead`. A program takes and returns all parts, laid end to end along the dimension named above; each array names one. Nothing has to cross between parts.
Inputs may be any that keep to these rules, and one draw needn't show every extreme that they name: `block_owner`: A permutation; the block in slot s is held by the device of index s along orb. dom_start[b] - 448 * block_owner[b] lies in 0 to 63. `pair_list`: each row names two different blocks whose slots differ by at most 2; no row repeats; a block is the first block of at most 3 rows, and some block of exactly 3.
All inputs are finite; a program needn't handle non-finite values.
Results may differ from a plain program's by a relative error of at most 0.00053.
Values may be sent and summed in bfloat16 or wider, within the bound.
A program may use at most 64 MiB of HBM per device.

v0:
```python
import jax
import jax.numpy as jnp
from jax import lax
from jax.sharding import PartitionSpec as P

RANGE = 2


def from_behind(value, axis, steps):
    count = lax.axis_size(axis)
    first, last = (max(0, -steps), min(count, count - steps))
    return lax.ppermute(value, axis, [(source, source + steps) for source in range(first, last)])


def block_in(block_owner, position):
    block_ids = jnp.arange(block_owner.shape[0], dtype=jnp.int32)
    return jnp.sum(jnp.where(block_owner == position, block_ids, 0))


def lookup(int_table, position):
    block_ids = jnp.arange(int_table.shape[0], dtype=jnp.int32)
    return jnp.sum(jnp.where(block_ids == position, int_table, 0))


def pair_term(window_all, coeff_block, offset):
    fit_count = window_all.shape[0]
    occ_count = window_all.shape[1]
    dom_count = coeff_block.shape[0]
    window = lax.dynamic_slice(
        window_all, (jnp.int32(0), jnp.int32(0), offset), (fit_count, occ_count, dom_count)
    )
    window = window.reshape(fit_count * occ_count, dom_count)
    fitted = jnp.dot(window, coeff_block, preferred_element_type=jnp.float32).astype(jnp.bfloat16)
    return lax.dot_general(
        window, fitted, (((0,), (0,)), ((), ())), preferred_element_type=jnp.float32
    )


def maybe_term(screened, local_ints, coeff_block, offset):
    empty = jnp.zeros((coeff_block.shape[0], coeff_block.shape[1]), jnp.float32)
    return lax.cond(screened, lambda: pair_term(local_ints, coeff_block, offset), lambda: empty)


def local(half_ints, orbital_coeffs, block_owner, dom_start, pair_list):
    my_place = lax.axis_index("orb")
    orb_count = lax.axis_size("orb")
    far_reach = min(RANGE, orb_count - 1)
    local_ints = half_ints[0]
    half_width = (local_ints.shape[2] - orbital_coeffs.shape[1]) // 2
    my_block = block_in(block_owner, my_place)
    my_start = lookup(dom_start, my_block)
    own_term = pair_term(local_ints, orbital_coeffs[0], my_start - my_start + half_width)
    shift_list = list(range(-far_reach, 0)) + list(range(1, far_reach + 1))
    neighbour = {}
    for shift_by in shift_list:
        neighbour[shift_by] = from_behind(orbital_coeffs, "orb", -shift_by)[0]
    pair_terms = {}
    for shift_by in shift_list:
        target = my_place + shift_by
        inside = (target >= 0) & (target < orb_count)
        partner = block_in(block_owner, target)
        listed = jnp.any((pair_list[:, 0] == my_block) & (pair_list[:, 1] == partner))
        offset = jnp.clip(lookup(dom_start, partner) - my_start + half_width, 0, 2 * half_width)
        pair_terms[shift_by] = maybe_term(inside & listed, local_ints, neighbour[shift_by], offset)
    summed = own_term
    for shift_by in shift_list:
        summed = summed + from_behind(pair_terms[shift_by], "orb", shift_by)
    result = lax.psum_scatter(summed, "fit", scatter_dimension=0, tiled=True)
    return result[None]


def solution(mesh):
    return jax.shard_map(
        local,
        mesh=mesh,
        in_specs=(
            P(("bead", "orb"), "fit", None, None),
            P(("bead", "orb"), None, None),
            P("bead"),
            P("bead"),
            P("bead", None),
        ),
        out_specs=P(("bead", "orb"), "fit", None),
        check_vma=False,
    )
```

profile of v0, /device:TPU:0, one launch (start us, length us, event | category | flops | bytes accessed | tf_op | source)
XLA Modules:
  0.0 106.2 jit_solution(7805687292265278015)
XLA Ops:
  6.5 0.0 reduce-scatter.2.cloned.1.call-start
  6.5 4.9 %collective-permute-start.2 = (bf16[1,512,128]{2,1,0:T(8,128)(2,1)}, bf16[1,512,128]{2,1,0:T(8,128)(2,1)S(1)}, u32[]{:S(2)}, u32[]{:S(2)}) collective-permute-start(bf16[1,512,128]{2,1,0:T(8,128)(2,1)} %param.14), channel_id=1, source_target_pairs={{0,4},{4,8},{8,12},{1,5},{5,9},{9,13},{2,6},{6,10},{10,14},{3,7},{... | collective-permute-start | bytes 393224 | tf_op jit(solution)/shard_map/ppermute | solution.py:12
  11.5 4.5 %collective-permute-start = (bf16[1,512,128]{2,1,0:T(8,128)(2,1)}, bf16[1,512,128]{2,1,0:T(8,128)(2,1)S(1)}, u32[]{:S(2)}, u32[]{:S(2)}) collective-permute-start(bf16[1,512,128]{2,1,0:T(8,128)(2,1)} %param.14), channel_id=1, source_target_pairs={{0,8},{4,12},{1,9},{5,13},{2,10},{6,14},{3,11},{7,15},{16,24},{20,... | collective-permute-start | bytes 393224 | tf_op jit(solution)/shard_map/ppermute | solution.py:12
  16.0 1.3 %collective-permute-start.6 = (bf16[1,512,128]{2,1,0:T(8,128)(2,1)}, bf16[1,512,128]{2,1,0:T(8,128)(2,1)S(1)}, u32[]{:S(2)}, u32[]{:S(2)}) collective-permute-start(bf16[1,512,128]{2,1,0:T(8,128)(2,1)} %param.14), channel_id=1, source_target_pairs={{8,0},{12,4},{9,1},{13,5},{10,2},{14,6},{11,3},{15,7},{24,16},{28,... | collective-permute-start | bytes 393224 | tf_op jit(solution)/shard_map/ppermute | solution.py:12
  17.3 1.3 %collective-permute-start.4 = (bf16[1,512,128]{2,1,0:T(8,128)(2,1)}, bf16[1,512,128]{2,1,0:T(8,128)(2,1)S(1)}, u32[]{:S(2)}, u32[]{:S(2)}) collective-permute-start(bf16[1,512,128]{2,1,0:T(8,128)(2,1)} %param.14), channel_id=1, source_target_pairs={{4,0},{8,4},{12,8},{5,1},{9,5},{13,9},{6,2},{10,6},{14,10},{7,3},{... | collective-permute-start | bytes 393224 | tf_op jit(solution)/shard_map/ppermute | solution.py:12
  18.6 1.5 %fusion.21 = (s32[]{:T(128)}, s32[]{:T(128)}, s32[]{:T(128)}, s32[]{:T(128)}, s32[]{:T(128)}) fusion(s32[4]{0:T(128)} %param.15, s32[]{:T(128)S(6)} %add.62, s32[]{:T(128)S(6)} %add.64, s32[]{:T(128)S(6)} %axis_index.15, s32[]{:T(128)S(6)} %add.68, s32[]{:T(128)S(6)} %add.66), kind=kLoop, calls=%fused_computation.40 | loop fusion | flops 55 | bytes 56 | tf_op jit(solution)/shard_map/reduce_sum | solution.py:17
  20.0 4.7 %and_reduce_fusion.3 = (pred[]{:T(512)}, pred[]{:T(512)}, pred[]{:T(512)}, pred[]{:T(512)}) fusion(s32[]{:T(128)} %get-tuple-element.241, s32[10,2]{0,1:T(2,128)} %param.17, s32[]{:T(128)} %get-tuple-element.244, s32[]{:T(128)} %get-tuple-element.245, s32[]{:T(128)} %get-tuple-element.242, s32[]{:T(128)} %get-tuple-element.243), kind=kLoop, calls=%fused_computation.36 | loop fusion | flops 126 | bytes 104 | tf_op jit(solution)/shard_map/reduce_or | solution.py:62
  27.2 1.8 %dynamic_slice.20 = bf16[8,128,512]{2,1,0:T(8,128)(2,1)S(1)} slice(bf16[8,128,2432]{2,1,0:T(8,128)(2,1)} %bitcast.44), slice={[0:8], [0:128], [960:1472]} | slice | bytes 2097152 | tf_op jit(solution)/shard_map/dynamic_slice | solution.py:29
  29.0 1.9 %fusion.22 = s32[]{:T(128)} fusion(s32[4]{0:T(128)} %param.16, s32[]{:T(128)} %get-tuple-element.243), kind=kLoop, calls=%fused_computation.41 | loop fusion | flops 11 | bytes 24 | tf_op jit(solution)/shard_map/reduce_sum | solution.py:22
  30.9 0.0 collective-permute-done.2
  30.9 0.1 copy.7
  31.1 0.0 collective-permute-done
  31.1 0.1 copy.6
  31.3 0.0 collective-permute-done.6
  31.3 0.0 copy-start
  31.3 6.0 %conditional.7 = (f32[512,128]{1,0:T(8,128)S(1)}) conditional(s32[]{:T(128)} %convert_element_type.35, () %tuple.43, (s32[]{:T(128)}, s32[4]{0:T(128)S(1)}, s32[4]{0:T(128)}, s32[4]{0:T(128)S(1)}, s32[]{:T(128)}, /*index=5*/bf16[8,128,2432]{2,1,0:T(8,128)(2,1)}, bf16[1,512,128]{2,1,0:T(8,128)(2,1)S(1)}) %tuple.64), branch_computations={%region_19.20_spmd, %region_20.22_spmd} | conditional | flops 268566528 | bytes 3539060 | solution.py:41
  31.3 1.9 %fusion.15 = s32[]{:T(128)} fusion(s32[4]{0:T(128)} %get-tuple-element.233, s32[4]{0:T(128)S(1)} %get-tuple-element.234, s32[4]{0:T(128)S(1)} %get-tuple-element.231, s32[]{:T(128)} %get-tuple-element.232), kind=kLoop, calls=%fused_computation.22 | loop fusion | flops 11 | bytes 56 | tf_op jit(solution)/shard_map/reduce_sum | solution.py:22
  34.4 1.8 %constant_dynamic-slice_fusion.3 = bf16[8,128,512]{2,1,0:T(8,128)(2,1)S(1)} fusion(bf16[8,128,2432]{2,1,0:T(8,128)(2,1)} %get-tuple-element.230, s32[]{:T(128)S(6)} %min.20), kind=kLoop, calls=%fused_computation.23 | loop fusion | bytes 2097156 | tf_op jit(solution)/shard_map/cond/branch_1_fun/dynamic_slice | solution.py:29
  36.2 1.1 %fusion.12 = f32[512,128]{1,0:T(8,128)S(1)} fusion(bf16[1024,512]{1,0:T(8,128)(2,1)S(1)} %bitcast.42, bf16[1,512,128]{2,1,0:T(8,128)(2,1)S(1)} %get-tuple-element.236), kind=kOutput, calls=%fused_computation.19 | convolution fusion | flops 268566528 | bytes 1441792 | tf_op jit(solution)/shard_map/cond/branch_1_fun/dot_general | solution.py:34
  37.4 0.1 copy.9
  37.5 0.0 collective-permute-done.4
  37.5 6.1 %conditional.6 = (f32[512,128]{1,0:T(8,128)S(1)}) conditional(s32[]{:T(128)} %convert_element_type.34, () %tuple.41, (s32[]{:T(128)}, s32[4]{0:T(128)S(1)}, s32[4]{0:T(128)}, s32[4]{0:T(128)S(1)}, s32[]{:T(128)}, /*index=5*/bf16[8,128,2432]{2,1,0:T(8,128)(2,1)}, bf16[1,512,128]{2,1,0:T(8,128)(2,1)S(1)}) %tuple.65), branch_computations={%region_14.15_spmd, %region_15.17_spmd} | conditional | flops 268566528 | bytes 3539060 | solution.py:41
  37.6 2.0 %fusion.11 = s32[]{:T(128)} fusion(s32[4]{0:T(128)} %get-tuple-element.226, s32[4]{0:T(128)S(1)} %get-tuple-element.227, s32[4]{0:T(128)S(1)} %get-tuple-element.224, s32[]{:T(128)} %get-tuple-element.225), kind=kLoop, calls=%fused_computation.16 | loop fusion | flops 11 | bytes 56 | tf_op jit(solution)/shard_map/reduce_sum | solution.py:22
  40.7 1.8 %constant_dynamic-slice_fusion.2 = bf16[8,128,512]{2,1,0:T(8,128)(2,1)S(1)} fusion(bf16[8,128,2432]{2,1,0:T(8,128)(2,1)} %get-tuple-element.223, s32[]{:T(128)S(6)} %min.19), kind=kLoop, calls=%fused_computation.17 | loop fusion | bytes 2097156 | tf_op jit(solution)/shard_map/cond/branch_1_fun/dynamic_slice | solution.py:29
  42.5 1.1 %fusion.8 = f32[512,128]{1,0:T(8,128)S(1)} fusion(bf16[1024,512]{1,0:T(8,128)(2,1)S(1)} %bitcast.43, bf16[1,512,128]{2,1,0:T(8,128)(2,1)S(1)} %get-tuple-element.229), kind=kOutput, calls=%fused_computation.13 | convolution fusion | flops 268566528 | bytes 1441792 | tf_op jit(solution)/shard_map/cond/branch_1_fun/dot_general | solution.py:34
  43.7 0.1 copy.8
  43.8 10.7 %collective-permute-start.5 = (f32[512,128]{0,1:T(8,128)S(1)}, f32[512,128]{0,1:T(8,128)S(1)}, u32[]{:S(2)}, u32[]{:S(2)}) collective-permute-start(f32[512,128]{0,1:T(8,128)S(1)} %copy.8), channel_id=1, source_target_pairs={{0,4},{4,8},{8,12},{1,5},{5,9},{9,13},{2,6},{6,10},{10,14},{3,7},{... | collective-permute-start | bytes 786440 | tf_op jit(solution)/shard_map/ppermute | solution.py:12
  54.5 3.6 %collective-permute-start.7 = (f32[512,128]{0,1:T(8,128)S(1)}, f32[512,128]{0,1:T(8,128)S(1)}, u32[]{:S(2)}, u32[]{:S(2)}) collective-permute-start(f32[512,128]{0,1:T(8,128)S(1)} %copy.9), channel_id=1, source_target_pairs={{0,8},{4,12},{1,9},{5,13},{2,10},{6,14},{3,11},{7,15},{16,24},{20,... | collective-permute-start | bytes 786440 | tf_op jit(solution)/shard_map/ppermute | solution.py:12
  58.1 1.3 %collective-permute-start.1 = (f32[512,128]{0,1:T(8,128)S(1)}, f32[512,128]{0,1:T(8,128)S(1)}, u32[]{:S(2)}, u32[]{:S(2)}) collective-permute-start(f32[512,128]{0,1:T(8,128)S(1)} %copy.6), channel_id=1, source_target_pairs={{8,0},{12,4},{9,1},{13,5},{10,2},{14,6},{11,3},{15,7},{24,16},{28,... | collective-permute-start | bytes 786440 | tf_op jit(solution)/shard_map/ppermute | solution.py:12
  59.4 1.3 %collective-permute-start.3 = (f32[512,128]{0,1:T(8,128)S(1)}, f32[512,128]{0,1:T(8,128)S(1)}, u32[]{:S(2)}, u32[]{:S(2)}) collective-permute-start(f32[512,128]{0,1:T(8,128)S(1)} %copy.7), channel_id=1, source_target_pairs={{4,0},{8,4},{12,8},{5,1},{9,5},{13,9},{6,2},{10,6},{14,10},{7,3},{... | collective-permute-start | bytes 786440 | tf_op jit(solution)/shard_map/ppermute | solution.py:12
  60.7 0.0 copy-done
  60.7 0.8 fusion.17
  61.5 0.0 collective-permute-done.5
  61.5 3.3 %collective-permute-done.7 = f32[512,128]{0,1:T(8,128)S(1)} collective-permute-done((f32[512,128]{0,1:T(8,128)S(1)}, f32[512,128]{0,1:T(8,128)S(1)}, u32[]{:S(2)}, u32[]{:S(2)}) %collective-permute-start.7) | collective-permute-done | bytes 262176 | tf_op jit(solution)/shard_map/ppermute | solution.py:12
  64.9 8.1 %collective-permute-done.1 = f32[512,128]{0,1:T(8,128)S(1)} collective-permute-done((f32[512,128]{0,1:T(8,128)S(1)}, f32[512,128]{0,1:T(8,128)S(1)}, u32[]{:S(2)}, u32[]{:S(2)}) %collective-permute-start.1) | collective-permute-done | bytes 262176 | tf_op jit(solution)/shard_map/ppermute | solution.py:12
  73.0 0.8 collective-permute-done.3
  73.8 0.8 add_add_fusion
  74.6 0.0 reduce-scatter.2.cloned.1.call-update
  74.7 23.1 %reduce-scatter.2.cloned.1.call-done = f32[128,128]{0,1:T(8,128)} async-done(((f32[512,128]{0,1:T(8,128)}), f32[128,128]{0,1:T(8,128)}) %reduce-scatter.2.cloned.1.call-update) | async-done | bytes 65552 | tf_op jit(solution)/shard_map/reduce_scatter | solution.py:68
  97.7 1.6 %copy.10 = f32[1,128,128]{2,1,0:T(8,128)} copy(f32[1,128,128]{1,2,0:T(8,128)} %bitcast.49) | data formatting | bytes 131072 | tf_op jit(solution)/shard_map/broadcast_in_dim | solution.py:69
  (9 shorter events, 0.1 us)
Async XLA Ops:
  6.5 91.2 %reduce-scatter.2.cloned.1.call-start = ((), (), s32[]{:S(2)}) async-start(), calls=%async_computation.1 | async-start | bytes 327680 | tf_op jit(solution)/shard_map/reduce_scatter | solution.py:68
  6.5 24.4 %collective-permute-start.2 = (bf16[1,512,128]{2,1,0:T(8,128)(2,1)}, bf16[1,512,128]{2,1,0:T(8,128)(2,1)S(1)}, u32[]{:S(2)}, u32[]{:S(2)}) collective-permute-start(bf16[1,512,128]{2,1,0:T(8,128)(2,1)} %param.14), channel_id=1, source_target_pairs={{0,4},{4,8},{8,12},{1,5},{5,9},{9,13},{2,6},{6,10},{10,14},{3,7},{... | collective-permute-start | bytes 393224 | tf_op jit(solution)/shard_map/ppermute | solution.py:12
  11.5 19.6 %collective-permute-start = (bf16[1,512,128]{2,1,0:T(8,128)(2,1)}, bf16[1,512,128]{2,1,0:T(8,128)(2,1)S(1)}, u32[]{:S(2)}, u32[]{:S(2)}) collective-permute-start(bf16[1,512,128]{2,1,0:T(8,128)(2,1)} %param.14), channel_id=1, source_target_pairs={{0,8},{4,12},{1,9},{5,13},{2,10},{6,14},{3,11},{7,15},{16,24},{20,... | collective-permute-start | bytes 393224 | tf_op jit(solution)/shard_map/ppermute | solution.py:12
  16.0 15.3 %collective-permute-start.6 = (bf16[1,512,128]{2,1,0:T(8,128)(2,1)}, bf16[1,512,128]{2,1,0:T(8,128)(2,1)S(1)}, u32[]{:S(2)}, u32[]{:S(2)}) collective-permute-start(bf16[1,512,128]{2,1,0:T(8,128)(2,1)} %param.14), channel_id=1, source_target_pairs={{8,0},{12,4},{9,1},{13,5},{10,2},{14,6},{11,3},{15,7},{24,16},{28,... | collective-permute-start | bytes 393224 | tf_op jit(solution)/shard_map/ppermute | solution.py:12
  17.3 20.2 %collective-permute-start.4 = (bf16[1,512,128]{2,1,0:T(8,128)(2,1)}, bf16[1,512,128]{2,1,0:T(8,128)(2,1)S(1)}, u32[]{:S(2)}, u32[]{:S(2)}) collective-permute-start(bf16[1,512,128]{2,1,0:T(8,128)(2,1)} %param.14), channel_id=1, source_target_pairs={{4,0},{8,4},{12,8},{5,1},{9,5},{13,9},{6,2},{10,6},{14,10},{7,3},{... | collective-permute-start | bytes 393224 | tf_op jit(solution)/shard_map/ppermute | solution.py:12
  31.3 29.4 %copy-start = (bf16[1,512,128]{2,1,0:T(8,128)(2,1)S(1)}, bf16[1,512,128]{2,1,0:T(8,128)(2,1)}, u32[]{:S(2)}) copy-start(bf16[1,512,128]{2,1,0:T(8,128)(2,1)} %param.14) | copy-start | bytes 393220
  43.8 17.7 %collective-permute-start.5 = (f32[512,128]{0,1:T(8,128)S(1)}, f32[512,128]{0,1:T(8,128)S(1)}, u32[]{:S(2)}, u32[]{:S(2)}) collective-permute-start(f32[512,128]{0,1:T(8,128)S(1)} %copy.8), channel_id=1, source_target_pairs={{0,4},{4,8},{8,12},{1,5},{5,9},{9,13},{2,6},{6,10},{10,14},{3,7},{... | collective-permute-start | bytes 786440 | tf_op jit(solution)/shard_map/ppermute | solution.py:12
  54.5 10.4 %collective-permute-start.7 = (f32[512,128]{0,1:T(8,128)S(1)}, f32[512,128]{0,1:T(8,128)S(1)}, u32[]{:S(2)}, u32[]{:S(2)}) collective-permute-start(f32[512,128]{0,1:T(8,128)S(1)} %copy.9), channel_id=1, source_target_pairs={{0,8},{4,12},{1,9},{5,13},{2,10},{6,14},{3,11},{7,15},{16,24},{20,... | collective-permute-start | bytes 786440 | tf_op jit(solution)/shard_map/ppermute | solution.py:12
  58.1 14.8 %collective-permute-start.1 = (f32[512,128]{0,1:T(8,128)S(1)}, f32[512,128]{0,1:T(8,128)S(1)}, u32[]{:S(2)}, u32[]{:S(2)}) collective-permute-start(f32[512,128]{0,1:T(8,128)S(1)} %copy.6), channel_id=1, source_target_pairs={{8,0},{12,4},{9,1},{13,5},{10,2},{14,6},{11,3},{15,7},{24,16},{28,... | collective-permute-start | bytes 786440 | tf_op jit(solution)/shard_map/ppermute | solution.py:12
  59.4 14.4 %collective-permute-start.3 = (f32[512,128]{0,1:T(8,128)S(1)}, f32[512,128]{0,1:T(8,128)S(1)}, u32[]{:S(2)}, u32[]{:S(2)}) collective-permute-start(f32[512,128]{0,1:T(8,128)S(1)} %copy.7), channel_id=1, source_target_pairs={{4,0},{8,4},{12,8},{5,1},{9,5},{13,9},{6,2},{10,6},{14,10},{7,3},{... | collective-permute-start | bytes 786440 | tf_op jit(solution)/shard_map/ppermute | solution.py:12
Sparse Core Ops, SparseCore 0:
  74.8 22.9 reduce-scatter.1
where the time goes:
time: 107 us; the launch traced here: 106 us
  waiting for transfers between devices  35.4 us (33%)
  starting transfers between devices  28.9 us (27%)
  between operations  16.1 us (15%)
  other arithmetic  12.7 us (12%)
  local copies, waits for them, and re-layouts  7.52 us (7%)
  matrix products  3.03 us (3%)
  loops' own time  2.51 us (2%)
    ppermute x8, starting transfers between devices, from_behind(): lax.ppermute(value, axis, [(source, source + steps) for source in range(f...  28.9 us
    reduce_scatter x1, waiting for transfers between devices, local(): result = lax.psum_scatter(summed, 'fit', scatter_dimension=0, tiled=True)  23.1 us
    ppermute x8, waiting for transfers between devices, from_behind(): lax.ppermute(value, axis, [(source, source + steps) for source in range(f...  12.3 us
    reduce_sum x3, other arithmetic, lookup(): return jnp.sum(jnp.where(block_ids == position, int_table, 0))  5.78 us
    dynamic_slice x3, local copies, waits for them, and re-layouts, pair_term(): lax.dynamic_slice(window_all, (jnp.int32(0), jnp.int32(0), offset), (fit_...  5.37 us
    reduce_or x1, other arithmetic, local(): jnp.any((pair_list[:, 0] == my_block) & (pair_list[:, 1] == partner))  4.67 us
    dot_general x3, matrix products, pair_term(): lax.dot_general(window, fitted, (((0,), (0,)), ((), ())), preferred_eleme...  3.03 us
    another operation x4, loops' own time, maybe_term(): lax.cond(screened, lambda: pair_term(local_ints, coeff_block, offset), la...  2.51 us
  transfers between devices with their start and end apart: 9, of which 4 were waited for; matrix products, arithmetic and copies ran while one was open for 15% of the time, Pallas kernels for 0%

commit v1 on v0

v1 whole, which is shorter than its diff:
```python
import functools

import jax
import jax.numpy as jnp
from jax import lax
from jax.experimental import pallas as pl
from jax.experimental.pallas import tpu as pltpu
from jax.sharding import PartitionSpec as P

MESH = pl.DeviceIdType.MESH
RANGE = 2
SPACING = 448
JIT = 64
LANE = 128
PAD = 192


def columns_of(shift, half, dom, win):
    low = (half + SPACING * shift - JIT + 1) // LANE * LANE
    high = -(-(half + SPACING * shift + JIT - 1 + dom) // LANE) * LANE
    if shift == 0:
        low, high = half // LANE * LANE, -(-(half + dom) // LANE) * LANE
    return max(low, 0), min(high, win)


def kernel(
    sizes, owner_ref, start_ref, pair_ref, ints_hbm, coeff_hbm, out_ref,
    ints, coeff, got, padded, wide, away, keep, got1, sum1, got2, sum2, got3,
    ints_sem, coeff_sem, csend, crecv, fsend, frecv, send1, recv1, send2, recv2, send3, recv3,
):
    orb_count, fit_count, reach = sizes
    shifts = [s for s in range(-reach, reach + 1) if s != 0]
    order = [0] + [sign * k for k in range(1, reach + 1) for sign in (-1, 1)]
    slot = {s: s + reach for s in range(-reach, reach + 1)}
    rows, win = ints.shape
    dom = 2 * coeff.shape[1]
    half = (win - dom) // 2
    quarter = out_ref.shape[0]
    me = lax.axis_index("orb")
    fit = lax.axis_index("fit")
    low = lax.rem(fit, 2)
    high = fit // 2
    pal1 = {"fit": high * 2 + 1 - low}
    pal2 = {"fit": (1 - high) * 2 + low}

    def inside(s):
        return (me + s >= 0) & (me + s < orb_count)

    def remote(src, dst, send, recv, device):
        return pltpu.make_async_remote_copy(
            src_ref=src, dst_ref=dst, send_sem=send, recv_sem=recv,
            device_id=device, device_id_type=MESH,
        )

    coeff_copy = pltpu.make_async_copy(coeff_hbm, coeff, coeff_sem)
    coeff_copy.start()
    spans = {s: columns_of(s, half, dom, win) for s in order}
    cuts = [spans[0]]
    for k in range(1, reach + 1):
        cuts = cuts + [(spans[-k][0], min(c[0] for c in cuts)), (max(c[1] for c in cuts), spans[k][1])]
    copies = []
    for n, (a, b) in enumerate(cuts):
        copy = pltpu.make_async_copy(ints_hbm.at[:, a:b], ints.at[:, a:b], ints_sem.at[n])
        copy.start()
        copies.append(copy)

    barrier = pltpu.get_barrier_semaphore()
    for pal in (pal1, pal2):
        pl.semaphore_signal(barrier, inc=1, device_id=pal, device_id_type=MESH)
    expected = jnp.int32(2)
    for s in shifts:
        @pl.when(inside(s))
        def _(s=s):
            pl.semaphore_signal(barrier, inc=1, device_id={"orb": me + s}, device_id_type=MESH)
        expected = expected + inside(s).astype(jnp.int32)

    zeros = jnp.zeros((PAD, padded.shape[1]), jnp.float32)
    padded[0:PAD] = zeros
    padded[PAD + dom : 2 * PAD + dom] = zeros

    blocks = owner_ref.shape[0]
    pairs = pair_ref.shape[0]
    wanted = list(range(-reach, reach + 1))

    def find(b, found):
        held = owner_ref[b]
        begin = start_ref[b]
        new = []
        for n, s in enumerate(wanted):
            hit = held == me + s
            new.append((jnp.where(hit, b, found[n][0]), jnp.where(hit, begin, found[n][1])))
        return tuple(new)

    found = tuple((jnp.int32(-1), jnp.int32(0)) for _ in wanted)
    found = lax.fori_loop(0, blocks, find, found, unroll=blocks <= 8)
    my_block, my_start = found[reach]

    def scan(p, listed):
        first = pair_ref[p, 0] == my_block
        second = pair_ref[p, 1]
        return tuple(
            jnp.where(first & (second == found[slot[s]][0]), 1, listed[n]) for n, s in enumerate(shifts)
        )

    listed = lax.fori_loop(0, pairs, scan, tuple(jnp.int32(0) for _ in shifts), unroll=pairs <= 16)
    listed = dict(zip(shifts, listed))

    pl.semaphore_wait(barrier, expected)

    coeff_out = {}
    for s in [k for k in order if k != 0]:
        coeff_out[s] = remote(
            coeff_hbm.at[low], got.at[slot[-s], low], csend.at[slot[s]], crecv.at[slot[-s]], {"orb": me + s}
        )

        @pl.when(inside(s))
        def _(s=s):
            coeff_out[s].start()

    def arrival(s):
        return remote(
            coeff_hbm.at[low], got.at[slot[s], low], csend.at[slot[-s]], crecv.at[slot[s]], {"orb": me + s}
        )

    def forward(s):
        return remote(got.at[slot[s], low], got.at[slot[s], low], fsend.at[slot[s]], frecv.at[slot[s]], pal1)

    def other_half(s):
        return remote(got.at[slot[s], low], got.at[slot[s], 1 - low], fsend.at[slot[s]], frecv.at[slot[s]], pal1)

    def stage1(s):
        n = slot[s]
        return remote(away.at[n], got1.at[n], send1.at[n], recv1.at[n], pal1)

    def stage2(s):
        n = slot[s]
        return remote(sum1.at[n, 1 - high], got2.at[n], send2.at[n], recv2.at[n], pal2)

    def stage3(s):
        return remote(sum2.at[slot[s]], got3.at[slot[-s]], send3.at[slot[s]], recv3.at[slot[-s]], {"orb": me + s})

    def compute(s):
        a, b = spans[s]
        width = b - a
        if s == 0:
            block = coeff[...]
            offset = jnp.int32(half - a)
        else:
            block = got[slot[s]]
            offset = jnp.clip(
                found[slot[s]][1] - my_start + half - a, max(0, width - dom - PAD), min(PAD, width - dom)
            )
        padded[PAD : PAD + dom] = block.reshape(dom, block.shape[-1]).astype(jnp.float32)
        shifted = padded[pl.ds(PAD - offset, width), :].astype(jnp.bfloat16)
        window = ints[:, a:b]
        fitted = jnp.dot(window, shifted, preferred_element_type=jnp.float32).astype(jnp.bfloat16)
        wide[0:width] = lax.dot_general(
            window, fitted, (((0,), (0,)), ((), ())), preferred_element_type=jnp.float32
        )
        for x in range(2):
            away[slot[s], x] = wide[pl.ds(offset + (2 * x + 1 - low) * quarter, quarter), :]
            keep[slot[s], x] = wide[pl.ds(offset + (2 * x + low) * quarter, quarter), :]

    def when(s, do):
        if s == 0:
            do()
        else:
            pl.when(inside(s))(do)

    def pass_on(s):
        def do():
            arrival(s).wait_recv()
            forward(s).start()
        when(s, do)

    def work(s):
        def do():
            if s != 0:
                other_half(s).wait_recv()
            compute(s)
            stage1(s).start()
        when(s, do)

    def first(s):
        def do():
            stage1(s).wait_recv()
            sum1[slot[s]] = keep[slot[s]] + got1[slot[s]]
            stage2(s).start()
        when(s, do)

    def second(s):
        def do():
            stage2(s).wait_recv()
            total = sum1[slot[s], high] + got2[slot[s]]
            if s == 0:
                sum2[slot[s]] = total
            else:
                sum2[slot[s]] = jnp.where(listed[s] > 0, total, 0.0)
                stage3(s).start()
        when(s, do)

    coeff_copy.wait()
    copies[0].wait()
    work(0)
    pass_on(-1)
    pass_on(1)
    first(0)
    waiting = []
    previous = 0
    for n, s in enumerate(order[1:]):
        copies[n + 1].wait()
        work(s)
        if s < 0 and abs(s) < reach:
            pass_on(s - 1)
            pass_on(1 - s)
        if previous != 0:
            first(previous)
        waiting.append(previous)
        if n >= 1:
            second(waiting[n - 1])
        previous = s
    first(previous)
    waiting.append(previous)
    for s in waiting[len(order) - 2 :]:
        second(s)

    total = sum2[slot[0]]
    out_ref[...] = total
    for s in shifts:
        def take(s=s):
            stage3(-s).wait_recv()
            out_ref[...] += got3[slot[s]]
        when(s, take)

    for s in order:
        def drain(s=s):
            stage1(s).wait_send()
            stage2(s).wait_send()
            if s != 0:
                coeff_out[s].wait_send()
                forward(s).wait_send()
                stage3(s).wait_send()
        when(s, drain)


def local(sizes, half_ints, orbital_coeffs, block_owner, dom_start, pair_list):
    orb_count, fit_count, reach = sizes
    _, fits, occ, win = half_ints.shape
    dom = orbital_coeffs.shape[1]
    ints = half_ints.reshape(fits * occ, win)
    coeffs = orbital_coeffs.reshape(2, dom // 2, occ)
    quarter = dom // fit_count
    slots = 2 * reach + 1
    f32 = jnp.float32
    dma = pltpu.SemaphoreType.DMA
    out = pl.pallas_call(
        functools.partial(kernel, sizes),
        out_shape=jax.ShapeDtypeStruct((quarter, occ), f32),
        in_specs=[pl.BlockSpec(memory_space=pltpu.SMEM)] * 3 + [pl.BlockSpec(memory_space=pl.ANY)] * 2,
        out_specs=pl.BlockSpec(memory_space=pltpu.VMEM),
        scratch_shapes=[
            pltpu.VMEM((fits * occ, win), jnp.bfloat16),
            pltpu.VMEM((2, dom // 2, occ), jnp.bfloat16),
            pltpu.VMEM((slots, 2, dom // 2, occ), jnp.bfloat16),
            pltpu.VMEM((2 * PAD + dom, occ), f32),
            pltpu.VMEM((dom + 256, occ), f32),
            pltpu.VMEM((slots, 2, quarter, occ), f32),
            pltpu.VMEM((slots, 2, quarter, occ), f32),
            pltpu.VMEM((slots, 2, quarter, occ), f32),
            pltpu.VMEM((slots, 2, quarter, occ), f32),
            pltpu.VMEM((slots, quarter, occ), f32),
            pltpu.VMEM((slots, quarter, occ), f32),
            pltpu.VMEM((slots, quarter, occ), f32),
            dma((slots,)),
            dma,
        ] + [dma((slots,))] * 10,
        compiler_params=pltpu.CompilerParams(
            collective_id=0, has_side_effects=True, vmem_limit_bytes=48 * 1024 * 1024
        ),
    )(block_owner, dom_start, pair_list, ints, coeffs)
    return out[None]


def solution(mesh):
    orb_count = mesh.shape["orb"]
    sizes = (orb_count, mesh.shape["fit"], min(RANGE, orb_count - 1))
    return jax.shard_map(
        functools.partial(local, sizes),
        mesh=mesh,
        in_specs=(
            P(("bead", "orb"), "fit", None, None),
            P(("bead", "orb"), None, None),
            P("bead"),
            P("bead"),
            P("bead", None),
        ),
        out_specs=P(("bead", "orb"), "fit", None),
        check_vma=False,
    )
```

time: 107 us -> 32.5 us (0.30)
  waiting for transfers between devices: 35.4 us -> 0 us
  starting transfers between devices: 28.9 us -> 0 us
  Pallas kernels: 0 us -> 26.3 us
  between operations: 16.1 us -> 0.01 us
  other arithmetic: 12.7 us -> 0 us
  matrix products: 3.03 us -> 0 us
  loops' own time: 2.51 us -> 0 us
  local copies, waits for them, and re-layouts: 7.52 us -> 6.02 us
    ppermute x8 -> x0, starting transfers between devices: 28.9 us -> none  [from_behind(): lax.ppermute(value, axis, [(source, source + steps) for source in range(f...]
    pallas_call x0 -> x1, Pallas kernels: none -> 26.3 us  [local(): pl.pallas_call(functools.partial(kernel, sizes), out_shape=jax.ShapeDtype...]
    reduce_scatter x1 -> x0, waiting for transfers between devices: 23.1 us -> none  [local(): result = lax.psum_scatter(summed, 'fit', scatter_dimension=0, tiled=True)]
    ppermute x8 -> x0, waiting for transfers between devices: 12.3 us -> none  [from_behind(): lax.ppermute(value, axis, [(source, source + steps) for source in range(f...]
    reduce_sum x4 -> x0, other arithmetic: 7.23 us -> none  [the longest x3 5.78 us: lookup(): return jnp.sum(jnp.where(block_ids == position, int_table, 0))]
    unnamed x2 -> x10, local copies, waits for them, and re-layouts: 0.01 us -> 6.02 us
    dynamic_slice x3 -> x0, local copies, waits for them, and re-layouts: 5.37 us -> none  [pair_term(): lax.dynamic_slice(window_all, (jnp.int32(0), jnp.int32(0), offset), (fit_...]
    reduce_or x1 -> x0, other arithmetic: 4.67 us -> none  [local(): jnp.any((pair_list[:, 0] == my_block) & (pair_list[:, 1] == partner))]
  transfers between devices with their start and end apart: 9 -> 0, of which waited for: 4 -> 0; matrix products, arithmetic and copies ran while one was open for 15% -> 0% of each run, Pallas kernels for 0% -> 0%
where the time goes in v1:
time: 32.5 us; the launch traced here: 32.3 us
  Pallas kernels  26.3 us (81%)
  local copies, waits for them, and re-layouts  6.02 us (19%)
    pallas_call x1, Pallas kernels, local(): pl.pallas_call(functools.partial(kernel, sizes), out_shape=jax.ShapeDtype...  26.3 us
    unnamed x10, local copies, waits for them, and re-layouts  6.02 us

profile of v1, /device:TPU:0, one launch (start us, length us, event | category | flops | bytes accessed | tf_op | source)
XLA Modules:
  0.0 32.3 jit_solution(7510176711520402671)
XLA Ops:
  0.0 0.8 %copy.6.pair_ref = s32[10,2]{1,0:T(8,128)S(1)} copy(s32[10,2]{0,1:T(2,128)} %param.9) | data formatting | bytes 160 | tf_op args[4]
  0.8 0.0 copy-start
  0.8 2.4 %copy-done = bf16[1,8,128,2432]{3,2,1,0:T(8,128)(2,1)S(1)} copy-done((bf16[1,8,128,2432]{3,2,1,0:T(8,128)(2,1)S(1)}, bf16[1,8,128,2432]{3,2,1,0:T(8,128)(2,1)}, u32[]{:S(2)}) %copy-start) | copy-done | bytes 4980760
  3.2 0.0 copy-start.1
  3.2 0.9 %copy-done.1 = bf16[1,512,128]{2,1,0:T(8,128)(2,1)S(1)} copy-done((bf16[1,512,128]{2,1,0:T(8,128)(2,1)S(1)}, bf16[1,512,128]{2,1,0:T(8,128)(2,1)}, u32[]{:S(2)}) %copy-start.1) | copy-done | bytes 131096
  4.1 0.0 copy-start.2
  4.1 0.7 %copy-done.2 = s32[4]{0:T(128)S(1)} copy-done((s32[4]{0:T(128)S(1)}, s32[4]{0:T(128)}, u32[]{:S(2)}) %copy-start.2) | copy-done | bytes 40
  4.7 0.0 copy-start.3
  4.7 0.7 %copy-done.3 = s32[4]{0:T(128)S(1)} copy-done((s32[4]{0:T(128)S(1)}, s32[4]{0:T(128)}, u32[]{:S(2)}) %copy-start.3) | copy-done | bytes 40
  5.4 26.3 %shard_map.55 = f32[128,128]{1,0:T(8,128)S(1)} custom-call(s32[4]{0:T(128)S(1)} %copy-done.2, s32[4]{0:T(128)S(1)} %copy-done.3, s32[10,2]{1,0:T(8,128)S(1)} %copy.6.pair_ref, bf16[1024,2432]{1,0:T(8,128)(2,1)S(1)} %bitcast.3, bf16[2,256,128]{2,1,0:T(8,128)(2,1)S(1)} %bitcast.5), custom_call_target="tpu_custom_call" | custom-call | tf_op jit(solution)/shard_map/pallas_call | solution.py:256
  31.7 0.6 %copy.8 = f32[1,128,128]{2,1,0:T(8,128)} copy(f32[1,128,128]{2,1,0:T(8,128)S(1)} %bitcast.4) | data formatting | bytes 131072
Async XLA Ops:
  0.8 2.4 %copy-start = (bf16[1,8,128,2432]{3,2,1,0:T(8,128)(2,1)S(1)}, bf16[1,8,128,2432]{3,2,1,0:T(8,128)(2,1)}, u32[]{:S(2)}) copy-start(bf16[1,8,128,2432]{3,2,1,0:T(8,128)(2,1)} %param.5) | copy-start | bytes 14942212
  3.2 0.9 %copy-start.1 = (bf16[1,512,128]{2,1,0:T(8,128)(2,1)S(1)}, bf16[1,512,128]{2,1,0:T(8,128)(2,1)}, u32[]{:S(2)}) copy-start(bf16[1,512,128]{2,1,0:T(8,128)(2,1)} %param.6) | copy-start | bytes 393220
  4.1 0.7 %copy-start.2 = (s32[4]{0:T(128)S(1)}, s32[4]{0:T(128)}, u32[]{:S(2)}) copy-start(s32[4]{0:T(128)} %owner_ref.1) | copy-start | bytes 52
  4.7 0.7 %copy-start.3 = (s32[4]{0:T(128)S(1)}, s32[4]{0:T(128)}, u32[]{:S(2)}) copy-start(s32[4]{0:T(128)} %start_ref.1) | copy-start | bytes 52

commit v2 on v1

--- a/solution.py
+++ b/solution.py
@@ -24,7 +24,8 @@
 
 
 def kernel(
-    sizes, owner_ref, start_ref, pair_ref, ints_hbm, coeff_hbm, out_ref,
+    sizes, owner_hbm, start_hbm, pair_hbm, ints_hbm, coeff_hbm, out_ref,
+    owner_ref, start_ref, pair_ref, table_sem,
     ints, coeff, got, padded, wide, away, keep, got1, sum1, got2, sum2, got3,
     ints_sem, coeff_sem, csend, crecv, fsend, frecv, send1, recv1, send2, recv2, send3, recv3,
 ):
@@ -52,6 +53,14 @@
             device_id=device, device_id_type=MESH,
         )
 
+    tables = [
+        pltpu.make_async_copy(src, dst, table_sem.at[n])
+        for n, (src, dst) in enumerate(
+            ((owner_hbm, owner_ref), (start_hbm, start_ref), (pair_hbm, pair_ref))
+        )
+    ]
+    for table in tables:
+        table.start()
     coeff_copy = pltpu.make_async_copy(coeff_hbm, coeff, coeff_sem)
     coeff_copy.start()
     spans = {s: columns_of(s, half, dom, win) for s in order}
@@ -78,8 +87,10 @@
     padded[0:PAD] = zeros
     padded[PAD + dom : 2 * PAD + dom] = zeros
 
+    for table in tables:
+        table.wait()
     blocks = owner_ref.shape[0]
-    pairs = pair_ref.shape[0]
+    pairs = pair_ref.shape[1]
     wanted = list(range(-reach, reach + 1))
 
     def find(b, found):
@@ -96,8 +107,8 @@
     my_block, my_start = found[reach]
 
     def scan(p, listed):
-        first = pair_ref[p, 0] == my_block
-        second = pair_ref[p, 1]
+        first = pair_ref[0, p] == my_block
+        second = pair_ref[1, p]
         return tuple(
             jnp.where(first & (second == found[slot[s]][0]), 1, listed[n]) for n, s in enumerate(shifts)
         )
@@ -256,9 +267,13 @@
     out = pl.pallas_call(
         functools.partial(kernel, sizes),
         out_shape=jax.ShapeDtypeStruct((quarter, occ), f32),
-        in_specs=[pl.BlockSpec(memory_space=pltpu.SMEM)] * 3 + [pl.BlockSpec(memory_space=pl.ANY)] * 2,
+        in_specs=[pl.BlockSpec(memory_space=pltpu.HBM)] * 5,
         out_specs=pl.BlockSpec(memory_space=pltpu.VMEM),
         scratch_shapes=[
+            pltpu.SMEM(block_owner.shape, jnp.int32),
+            pltpu.SMEM(dom_start.shape, jnp.int32),
+            pltpu.SMEM(pair_list.shape[::-1], jnp.int32),
+            dma((3,)),
             pltpu.VMEM((fits * occ, win), jnp.bfloat16),
             pltpu.VMEM((2, dom // 2, occ), jnp.bfloat16),
             pltpu.VMEM((slots, 2, dom // 2, occ), jnp.bfloat16),
@@ -275,9 +290,9 @@
             dma,
         ] + [dma((slots,))] * 10,
         compiler_params=pltpu.CompilerParams(
-            collective_id=0, has_side_effects=True, vmem_limit_bytes=48 * 1024 * 1024
+            collective_id=0, has_side_effects=True, vmem_limit_bytes=64 * 1024 * 1024
         ),
-    )(block_owner, dom_start, pair_list, ints, coeffs)
+    )(block_owner, dom_start, pair_list.T, ints, coeffs)
     return out[None]
 
 

time: 32.5 us -> 27.5 us (0.85)
  local copies, waits for them, and re-layouts: 6.02 us -> 1.47 us
  Pallas kernels: 26.3 us -> 25.8 us
    unnamed x10 -> x1, local copies, waits for them, and re-layouts: 6.02 us -> 1.47 us
    pallas_call x1, Pallas kernels: 26.3 us -> 25.8 us  [local(): pl.pallas_call(functools.partial(kernel, sizes), out_shape=jax.ShapeDtype...]
where the time goes in v2:
time: 27.5 us; the launch traced here: 27.3 us
  Pallas kernels  25.8 us (94%)
  local copies, waits for them, and re-layouts  1.47 us (5%)
    pallas_call x1, Pallas kernels, local(): pl.pallas_call(functools.partial(kernel, sizes), out_shape=jax.ShapeDtype...  25.8 us
    unnamed x1, local copies, waits for them, and re-layouts  1.47 us

profile of v2, /device:TPU:0, one launch (start us, length us, event | category | flops | bytes accessed | tf_op | source)
XLA Modules:
  0.0 27.3 jit_solution(9771488805653626149)
XLA Ops:
  0.0 25.8 %shard_map.55 = f32[128,128]{1,0:T(8,128)} custom-call(s32[4]{0:T(128)} %owner_hbm.1, s32[4]{0:T(128)} %start_hbm.1, s32[2,10]{1,0:T(2,128)} %bitcast.7, bf16[1024,2432]{1,0:T(8,128)(2,1)} %bitcast.4, bf16[2,256,128]{2,1,0:T(8,128)(2,1)} %bitcast.6), custom_call_target="tpu_custom_call" | custom-call | tf_op jit(solution)/shard_map/pallas_call | solution.py:267
  25.9 1.5 %copy.7 = f32[1,128,128]{2,1,0:T(8,128)} copy(f32[1,128,128]{2,1,0:T(8,128)} %bitcast.5) | data formatting | bytes 131072

commit v3 on v2

--- a/solution.py
+++ b/solution.py
@@ -31,7 +31,7 @@
 ):
     orb_count, fit_count, reach = sizes
     shifts = [s for s in range(-reach, reach + 1) if s != 0]
-    order = [0] + [sign * k for k in range(1, reach + 1) for sign in (-1, 1)]
+    order = [0] + [sign * k for k in range(reach, 0, -1) for sign in (-1, 1)]
     slot = {s: s + reach for s in range(-reach, reach + 1)}
     rows, win = ints.shape
     dom = 2 * coeff.shape[1]
@@ -164,10 +164,10 @@
         padded[PAD : PAD + dom] = block.reshape(dom, block.shape[-1]).astype(jnp.float32)
         shifted = padded[pl.ds(PAD - offset, width), :].astype(jnp.bfloat16)
         window = ints[:, a:b]
-        fitted = jnp.dot(window, shifted, preferred_element_type=jnp.float32).astype(jnp.bfloat16)
-        wide[0:width] = lax.dot_general(
-            window, fitted, (((0,), (0,)), ((), ())), preferred_element_type=jnp.float32
-        )
+        fitted = lax.dot_general(
+            shifted, window, (((0,), (1,)), ((), ())), preferred_element_type=jnp.float32
+        ).astype(jnp.bfloat16)
+        wide[0:width] = jnp.dot(fitted, window, preferred_element_type=jnp.float32).T
         for x in range(2):
             away[slot[s], x] = wide[pl.ds(offset + (2 * x + 1 - low) * quarter, quarter), :]
             keep[slot[s], x] = wide[pl.ds(offset + (2 * x + low) * quarter, quarter), :]
@@ -213,26 +213,21 @@
     coeff_copy.wait()
     copies[0].wait()
     work(0)
-    pass_on(-1)
-    pass_on(1)
+    for s in order[1:3]:
+        pass_on(s)
     first(0)
-    waiting = []
-    previous = 0
+    for copy in copies[1:]:
+        copy.wait()
     for n, s in enumerate(order[1:]):
-        copies[n + 1].wait()
         work(s)
-        if s < 0 and abs(s) < reach:
-            pass_on(s - 1)
-            pass_on(1 - s)
-        if previous != 0:
-            first(previous)
-        waiting.append(previous)
-        if n >= 1:
-            second(waiting[n - 1])
-        previous = s
-    first(previous)
-    waiting.append(previous)
-    for s in waiting[len(order) - 2 :]:
+        if n + 3 < len(order):
+            pass_on(order[n + 3])
+        if n > 0:
+            first(order[n])
+    second(order[1])
+    second(order[2])
+    first(order[-1])
+    for s in order[3:] + [0]:
         second(s)
 
     total = sum2[slot[0]]

time: 27.5 us -> 24 us (0.87)
  Pallas kernels: 25.8 us -> 22.4 us
    pallas_call x1, Pallas kernels: 25.8 us -> 22.4 us  [local(): pl.pallas_call(functools.partial(kernel, sizes), out_shape=jax.ShapeDtype...]
where the time goes in v3:
time: 24 us; the launch traced here: 23.9 us
  Pallas kernels  22.4 us (93%)
  local copies, waits for them, and re-layouts  1.47 us (6%)
    pallas_call x1, Pallas kernels, local(): pl.pallas_call(functools.partial(kernel, sizes), out_shape=jax.ShapeDtype...  22.4 us
    unnamed x1, local copies, waits for them, and re-layouts  1.47 us

profile of v3, /device:TPU:0, one launch (start us, length us, event | category | flops | bytes accessed | tf_op | source)
XLA Modules:
  0.0 23.9 jit_solution(12526374099600027265)
XLA Ops:
  0.0 22.4 %shard_map.55 = f32[128,128]{1,0:T(8,128)} custom-call(s32[4]{0:T(128)} %owner_hbm.1, s32[4]{0:T(128)} %start_hbm.1, s32[2,10]{1,0:T(2,128)} %bitcast.7, bf16[1024,2432]{1,0:T(8,128)(2,1)} %bitcast.4, bf16[2,256,128]{2,1,0:T(8,128)(2,1)} %bitcast.6), custom_call_target="tpu_custom_call" | custom-call | tf_op jit(solution)/shard_map/pallas_call | solution.py:262
  22.4 1.5 %copy.7 = f32[1,128,128]{2,1,0:T(8,128)} copy(f32[1,128,128]{2,1,0:T(8,128)} %bitcast.5) | data formatting | bytes 131072

commit v4 on v3

--- a/solution.py
+++ b/solution.py
@@ -8,6 +8,8 @@
 from jax.sharding import PartitionSpec as P
 
 MESH = pl.DeviceIdType.MESH
+STEPS = 16384.0
+TAIL = 16
 RANGE = 2
 SPACING = 448
 JIT = 64
@@ -26,7 +28,7 @@
 def kernel(
     sizes, owner_hbm, start_hbm, pair_hbm, ints_hbm, coeff_hbm, out_ref,
     owner_ref, start_ref, pair_ref, table_sem,
-    ints, coeff, got, padded, wide, away, keep, got1, sum1, got2, sum2, got3,
+    ints, coeff, got, padded, wide, away, keep, got1, sum1, got2, coded, got3,
     ints_sem, coeff_sem, csend, crecv, fsend, frecv, send1, recv1, send2, recv2, send3, recv3,
 ):
     orb_count, fit_count, reach = sizes
@@ -81,7 +83,9 @@
         @pl.when(inside(s))
         def _(s=s):
             pl.semaphore_signal(barrier, inc=1, device_id={"orb": me + s}, device_id_type=MESH)
-        expected = expected + inside(s).astype(jnp.int32)
+            far = {"orb": me + s, "fit": pal2["fit"]}
+            pl.semaphore_signal(barrier, inc=1, device_id=far, device_id_type=MESH)
+        expected = expected + 2 * inside(s).astype(jnp.int32)
 
     zeros = jnp.zeros((PAD, padded.shape[1]), jnp.float32)
     padded[0:PAD] = zeros
@@ -143,12 +147,30 @@
         n = slot[s]
         return remote(away.at[n], got1.at[n], send1.at[n], recv1.at[n], pal1)
 
-    def stage2(s):
-        n = slot[s]
-        return remote(sum1.at[n, 1 - high], got2.at[n], send2.at[n], recv2.at[n], pal2)
-
-    def stage3(s):
-        return remote(sum2.at[slot[s]], got3.at[slot[-s]], send3.at[slot[s]], recv3.at[slot[-s]], {"orb": me + s})
+    def stage2():
+        return remote(sum1.at[1 - high], got2, send2, recv2, pal2)
+
+    def stage3(s, across=0):
+        return remote(
+            coded.at[slot[s], 1 - high if across else high], got3.at[slot[-s], across],
+            send3.at[slot[s], across], recv3.at[slot[-s], across],
+            {"orb": me + s, "fit": pal2["fit"] if across else fit},
+        )
+
+    def encode(value):
+        peak = jnp.maximum(jnp.max(jnp.abs(value), axis=0, keepdims=True), 1e-37)
+        level = jnp.clip(jnp.ceil(jnp.log2(peak)), -126.0, 127.0)
+        part = jnp.floor(level * 0.5)
+        steps = value * jnp.exp2(-part) * (jnp.exp2(part - level) * STEPS)
+        steps = jnp.clip(jnp.floor(steps + 0.5), -32767.0, 32767.0)
+        tail = jnp.broadcast_to(level, (TAIL, value.shape[1]))
+        return steps.astype(jnp.int32).astype(jnp.int16), tail.astype(jnp.int32).astype(jnp.int16)
+
+    def decode(ref):
+        level = ref[quarter : quarter + TAIL].astype(jnp.int32).astype(jnp.float32)[0:1]
+        part = jnp.floor(level * 0.5)
+        steps = ref[0:quarter].astype(jnp.int32).astype(jnp.float32)
+        return steps * (jnp.exp2(level - part) * (1.0 / STEPS)) * jnp.exp2(part)
 
     def compute(s):
         a, b = spans[s]
@@ -195,19 +217,16 @@
     def first(s):
         def do():
             stage1(s).wait_recv()
-            sum1[slot[s]] = keep[slot[s]] + got1[slot[s]]
-            stage2(s).start()
-        when(s, do)
-
-    def second(s):
-        def do():
-            stage2(s).wait_recv()
-            total = sum1[slot[s], high] + got2[slot[s]]
             if s == 0:
-                sum2[slot[s]] = total
-            else:
-                sum2[slot[s]] = jnp.where(listed[s] > 0, total, 0.0)
-                stage3(s).start()
+                sum1[...] = keep[slot[s]] + got1[slot[s]]
+                stage2().start()
+                return
+            for across in (1, 0):
+                x = 1 - high if across else high
+                total = keep[slot[s], x] + got1[slot[s], x]
+                total = jnp.where(listed[s] > 0, total, 0.0)
+                coded[slot[s], x, 0:quarter], coded[slot[s], x, quarter : quarter + TAIL] = encode(total)
+                stage3(s, across).start()
         when(s, do)
 
     coeff_copy.wait()
@@ -224,28 +243,26 @@
             pass_on(order[n + 3])
         if n > 0:
             first(order[n])
-    second(order[1])
-    second(order[2])
     first(order[-1])
-    for s in order[3:] + [0]:
-        second(s)
-
-    total = sum2[slot[0]]
-    out_ref[...] = total
-    for s in shifts:
+    stage2().wait_recv()
+    out_ref[...] = sum1[high] + got2[...]
+    for s in order[1:]:
         def take(s=s):
-            stage3(-s).wait_recv()
-            out_ref[...] += got3[slot[s]]
+            for across in (0, 1):
+                stage3(-s, across).wait_recv()
+                out_ref[...] += decode(got3.at[slot[s], across])
         when(s, take)
 
     for s in order:
         def drain(s=s):
             stage1(s).wait_send()
-            stage2(s).wait_send()
-            if s != 0:
+            if s == 0:
+                stage2().wait_send()
+            else:
                 coeff_out[s].wait_send()
                 forward(s).wait_send()
                 stage3(s).wait_send()
+                stage3(s, 1).wait_send()
         when(s, drain)
 
 
@@ -277,13 +294,13 @@
             pltpu.VMEM((slots, 2, quarter, occ), f32),
             pltpu.VMEM((slots, 2, quarter, occ), f32),
             pltpu.VMEM((slots, 2, quarter, occ), f32),
-            pltpu.VMEM((slots, 2, quarter, occ), f32),
-            pltpu.VMEM((slots, quarter, occ), f32),
-            pltpu.VMEM((slots, quarter, occ), f32),
-            pltpu.VMEM((slots, quarter, occ), f32),
+            pltpu.VMEM((2, quarter, occ), f32),
+            pltpu.VMEM((quarter, occ), f32),
+            pltpu.VMEM((slots, 2, quarter + TAIL, occ), jnp.int16),
+            pltpu.VMEM((slots, 2, quarter + TAIL, occ), jnp.int16),
             dma((slots,)),
             dma,
-        ] + [dma((slots,))] * 10,
+        ] + [dma((slots,))] * 6 + [dma, dma] + [dma((slots, 2))] * 2,
         compiler_params=pltpu.CompilerParams(
             collective_id=0, has_side_effects=True, vmem_limit_bytes=64 * 1024 * 1024
         ),

time: 24 us -> 20.5 us (0.85)
  Pallas kernels: 22.4 us -> 18.8 us
    pallas_call x1, Pallas kernels: 22.4 us -> 18.8 us  [local(): pl.pallas_call(functools.partial(kernel, sizes), out_shape=jax.ShapeDtype...]
where the time goes in v4:
time: 20.5 us; the launch traced here: 20.3 us
  Pallas kernels  18.8 us (92%)
  local copies, waits for them, and re-layouts  1.47 us (7%)
    pallas_call x1, Pallas kernels, local(): pl.pallas_call(functools.partial(kernel, sizes), out_shape=jax.ShapeDtype...  18.8 us
    unnamed x1, local copies, waits for them, and re-layouts  1.47 us

profile of v4, /device:TPU:0, one launch (start us, length us, event | category | flops | bytes accessed | tf_op | source)
XLA Modules:
  0.0 20.3 jit_solution(4092024362182294770)
XLA Ops:
  0.0 18.8 %shard_map.55 = f32[128,128]{1,0:T(8,128)} custom-call(s32[4]{0:T(128)} %owner_hbm.1, s32[4]{0:T(128)} %start_hbm.1, s32[2,10]{1,0:T(2,128)} %bitcast.7, bf16[1024,2432]{1,0:T(8,128)(2,1)} %bitcast.4, bf16[2,256,128]{2,1,0:T(8,128)(2,1)} %bitcast.6), custom_call_target="tpu_custom_call" | custom-call | tf_op jit(solution)/shard_map/pallas_call | solution.py:279
  18.8 1.5 %copy.7 = f32[1,128,128]{2,1,0:T(8,128)} copy(f32[1,128,128]{2,1,0:T(8,128)} %bitcast.5) | data formatting | bytes 131072

commit v5 on v4

--- a/solution.py
+++ b/solution.py
@@ -55,6 +55,18 @@
             device_id=device, device_id_type=MESH,
         )
 
+    barrier = pltpu.get_barrier_semaphore()
+    for pal in (pal1, pal2):
+        pl.semaphore_signal(barrier, inc=1, device_id=pal, device_id_type=MESH)
+    expected = jnp.int32(2)
+    for s in shifts:
+        @pl.when(inside(s))
+        def _(s=s):
+            pl.semaphore_signal(barrier, inc=1, device_id={"orb": me + s}, device_id_type=MESH)
+            far = {"orb": me + s, "fit": pal2["fit"]}
+            pl.semaphore_signal(barrier, inc=1, device_id=far, device_id_type=MESH)
+        expected = expected + 2 * inside(s).astype(jnp.int32)
+
     tables = [
         pltpu.make_async_copy(src, dst, table_sem.at[n])
         for n, (src, dst) in enumerate(
@@ -75,17 +87,17 @@
         copy.start()
         copies.append(copy)
 
-    barrier = pltpu.get_barrier_semaphore()
-    for pal in (pal1, pal2):
-        pl.semaphore_signal(barrier, inc=1, device_id=pal, device_id_type=MESH)
-    expected = jnp.int32(2)
-    for s in shifts:
+    pl.semaphore_wait(barrier, expected)
+
+    coeff_out = {}
+    for s in [k for k in order if k != 0]:
+        coeff_out[s] = remote(
+            coeff_hbm.at[low], got.at[slot[-s], low], csend.at[slot[s]], crecv.at[slot[-s]], {"orb": me + s}
+        )
+
         @pl.when(inside(s))
         def _(s=s):
-            pl.semaphore_signal(barrier, inc=1, device_id={"orb": me + s}, device_id_type=MESH)
-            far = {"orb": me + s, "fit": pal2["fit"]}
-            pl.semaphore_signal(barrier, inc=1, device_id=far, device_id_type=MESH)
-        expected = expected + 2 * inside(s).astype(jnp.int32)
+            coeff_out[s].start()
 
     zeros = jnp.zeros((PAD, padded.shape[1]), jnp.float32)
     padded[0:PAD] = zeros
@@ -120,18 +132,6 @@
     listed = lax.fori_loop(0, pairs, scan, tuple(jnp.int32(0) for _ in shifts), unroll=pairs <= 16)
     listed = dict(zip(shifts, listed))
 
-    pl.semaphore_wait(barrier, expected)
-
-    coeff_out = {}
-    for s in [k for k in order if k != 0]:
-        coeff_out[s] = remote(
-            coeff_hbm.at[low], got.at[slot[-s], low], csend.at[slot[s]], crecv.at[slot[-s]], {"orb": me + s}
-        )
-
-        @pl.when(inside(s))
-        def _(s=s):
-            coeff_out[s].start()
-
     def arrival(s):
         return remote(
             coeff_hbm.at[low], got.at[slot[s], low], csend.at[slot[-s]], crecv.at[slot[s]], {"orb": me + s}
@@ -170,7 +170,7 @@
         level = ref[quarter : quarter + TAIL].astype(jnp.int32).astype(jnp.float32)[0:1]
         part = jnp.floor(level * 0.5)
         steps = ref[0:quarter].astype(jnp.int32).astype(jnp.float32)
-        return steps * (jnp.exp2(level - part) * (1.0 / STEPS)) * jnp.exp2(part)
+        return steps * jnp.exp2(level - part) * jnp.exp2(part)
 
     def compute(s):
         a, b = spans[s]
@@ -245,7 +245,7 @@
             first(order[n])
     first(order[-1])
     stage2().wait_recv()
-    out_ref[...] = sum1[high] + got2[...]
+    out_ref[...] = (sum1[high] + got2[...]) * STEPS
     for s in order[1:]:
         def take(s=s):
             for across in (0, 1):
@@ -305,7 +305,7 @@
             collective_id=0, has_side_effects=True, vmem_limit_bytes=64 * 1024 * 1024
         ),
     )(block_owner, dom_start, pair_list.T, ints, coeffs)
-    return out[None]
+    return out[None] * (1.0 / STEPS)
 
 
 def solution(mesh):

time: 20.5 us -> 20.4 us (level)
  other arithmetic: 0 us -> 1.48 us
  local copies, waits for them, and re-layouts: 1.47 us -> 0 us
    mul x0 -> x1, other arithmetic: none -> 1.48 us  [local(): return out[None] * (1.0 / STEPS)]
    unnamed x1 -> x0, local copies, waits for them, and re-layouts: 1.47 us -> none
where the time goes in v5:
time: 20.4 us; the launch traced here: 20.3 us
  Pallas kernels  18.8 us (92%)
  other arithmetic  1.48 us (7%)
    pallas_call x1, Pallas kernels, local(): pl.pallas_call(functools.partial(kernel, sizes), out_shape=jax.ShapeDtype...  18.8 us
    mul x1, other arithmetic, local(): return out[None] * (1.0 / STEPS)  1.48 us

profile of v5, /device:TPU:0, one launch (start us, length us, event | category | flops | bytes accessed | tf_op | source)
XLA Modules:
  0.0 20.3 jit_solution(4239082483624706650)
XLA Ops:
  0.0 18.8 %shard_map.55 = f32[128,128]{1,0:T(8,128)} custom-call(s32[4]{0:T(128)} %owner_hbm.1, s32[4]{0:T(128)} %start_hbm.1, s32[2,10]{1,0:T(2,128)} %bitcast.7, bf16[1024,2432]{1,0:T(8,128)(2,1)} %bitcast.5, bf16[2,256,128]{2,1,0:T(8,128)(2,1)} %bitcast.6), custom_call_target="tpu_custom_call" | custom-call | tf_op jit(solution)/shard_map/pallas_call | solution.py:279
  18.8 1.5 %multiply_bitcast_fusion = f32[1,128,128]{2,1,0:T(8,128)} fusion(f32[128,128]{1,0:T(8,128)} %shard_map.55), kind=kLoop, calls=%fused_computation | loop fusion | flops 16384 | bytes 131072 | tf_op jit(solution)/shard_map/mul | solution.py:308
